TPU v7x, 128 devices: a whole 4x4x4 slice. The times are simulated.
128 devices in a mesh: tm: 8 (over x, core), sy: 4 (over z), sx: 4 (over y).
Axes of the slice: x: 4, y: 4, z: 4, core: 2. Of those that a mesh axis runs over, the one named last changes fastest.
Arguments:
- latent_init: float32 [64, 96, 320], P('sy', 'sx'), may hold values from -80 to 80
- step_noise: bfloat16 [32, 64, 96, 320], P('tm', 'sy', 'sx'), may hold values from -6 to 6
- coef_state: float32 [32], P('tm'), may hold values from -0.06 to -0.01
- coef_drift: float32 [32], P('tm'), may hold values from -0.1 to 0.1
- coef_noise: float32 [32], P('tm'), may hold values from 0.05 to 0.2
- step_index: int32 [32], P('tm'), may hold values from 0 to 999
- time_table: float32 [1000, 320], replicated, may hold values from -1.5 to 1.5
- norm_gain: float32 [320], replicated, may hold values from 0.25 to 1.75
- conv_weight: bfloat16 [3, 3, 320, 320], replicated, may hold values from -0.109375 to 0.109375
- reward_grad: float32 [64, 96, 320], P('sy', 'sx'), may hold values from -0.18 to 0.18
Outputs:
- trajectory: float32 [32, 64, 96, 320], P('tm', 'sy', 'sx')
- grad_weight: float32 [3, 3, 320, 320], P(None, None, None, 'tm')
All inputs are finite; a program needn't handle non-finite values.
Results may differ from a plain program's by a relative error of at most 0.0009.
The roundings to bfloat16 on the way count: a program that leaves them out, or rounds other values in their place, can miss the bound.
Values may be sent and summed in bfloat16 or wider, within the bound.
A program may use at most 128 MiB of HBM per device.

v0:
```python
import jax
import jax.numpy as jnp
from jax import lax
from jax.sharding import PartitionSpec as P

GROUPS = 32
ITERS = 2
EPSILON = 1e-05


def prefix(value, axis, join, neutral, backward):
    count, mine = (lax.axis_size(axis), lax.axis_index(axis))
    pieces = lax.all_gather(value, axis)
    if backward:
        pieces = pieces[::-1]
        mine = count - 1 - mine
    subtotal = jnp.full_like(value, 0) + jnp.asarray(neutral, value.dtype)

    def step(position, subtotal):
        longer = join(subtotal, pieces[position])
        return jnp.where(position < mine, longer, subtotal)

    return lax.fori_loop(0, count - 1, step, subtotal)


def with_halo(block, sides, width):
    for axis, dim in sides:
        count = lax.axis_size(axis)
        forward = [(i, i + 1) for i in range(count - 1)]
        backward = [(target, source) for source, target in forward]
        low = lax.ppermute(
            lax.slice_in_dim(block, block.shape[dim] - width, None, axis=dim), axis, forward
        )
        high = lax.ppermute(lax.slice_in_dim(block, 0, width, axis=dim), axis, backward)
        block = jnp.concatenate([low, block, high], axis=dim)
    return block


def add_terms(earlier, later):
    return earlier + later


def lower_total(block_total, reverse):
    return prefix(block_total, "tm", add_terms, jnp.zeros_like(block_total), reverse)


def group_count(tile_rows, tile_cols, channels):
    return tile_rows * lax.axis_size("sy") * tile_cols * lax.axis_size("sx") * (channels // GROUPS)


def group_stats(grouped, cell_count):
    totals = lax.psum(jnp.sum(grouped, axis=(1, 3)), ("sy", "sx"))
    center = totals / cell_count
    shifted = grouped - center[:, None, :, None]
    spread = lax.psum(jnp.sum(shifted * shifted, axis=(1, 3)), ("sy", "sx")) / cell_count
    return (shifted, spread)


def prepare(states, modulate):
    steps_here, tile_rows, tile_cols, channels = states.shape
    grouped = states.reshape(steps_here, tile_rows * tile_cols, GROUPS, channels // GROUPS)
    shifted, spread = group_stats(grouped, group_count(tile_rows, tile_cols, channels))
    inv_std = 1.0 / jnp.sqrt(spread + EPSILON)
    normal_field = (shifted * inv_std[:, None, :, None]).reshape(states.shape)
    pre_act = normal_field * modulate[:, None, None, :]
    activation = jax.nn.silu(pre_act).astype(jnp.bfloat16)
    act_pad = with_halo(activation, (("sy", 1), ("sx", 2)), 1)
    return (normal_field, inv_std, pre_act, act_pad)


def convolve(act_pad, conv_weight, tile_rows, tile_cols):
    result = jnp.zeros(
        act_pad.shape[:1] + (tile_rows, tile_cols, conv_weight.shape[3]), jnp.float32
    )
    for row_off in range(3):
        for col_off in range(3):
            window = act_pad[:, row_off : row_off + tile_rows, col_off : col_off + tile_cols, :]
            result = result + jnp.einsum(
                "bhwc,cd->bhwd",
                window,
                conv_weight[row_off, col_off],
                preferred_element_type=jnp.float32,
            )
    return result


def backprop(upstream, act_cache, modulate, conv_weight, need_state):
    normal_field, inv_std, pre_act, act_pad = act_cache
    steps_here, tile_rows, tile_cols, channels = upstream.shape
    up_half = upstream.astype(jnp.bfloat16)
    weight_rows = []
    for row_off in range(3):
        weight_cols = []
        for col_off in range(3):
            window = act_pad[:, row_off : row_off + tile_rows, col_off : col_off + tile_cols, :]
            weight_cols.append(
                jnp.einsum("bhwc,bhwd->cd", window, up_half, preferred_element_type=jnp.float32)
            )
        weight_rows.append(jnp.stack(weight_cols))
    grad_piece = jnp.stack(weight_rows)
    if not need_state:
        return (upstream, grad_piece)
    up_pad = with_halo(up_half, (("sy", 1), ("sx", 2)), 1)
    d_act = jnp.zeros(upstream.shape, jnp.float32)
    for row_off in range(3):
        for col_off in range(3):
            window = up_pad[
                :, 2 - row_off : 2 - row_off + tile_rows, 2 - col_off : 2 - col_off + tile_cols, :
            ]
            d_act = d_act + jnp.einsum(
                "bhwd,cd->bhwc",
                window,
                conv_weight[row_off, col_off],
                preferred_element_type=jnp.float32,
            )
    sig_value = jax.nn.sigmoid(pre_act)
    d_norm = d_act * sig_value * (1.0 + pre_act * (1.0 - sig_value)) * modulate[:, None, None, :]
    group_shape = (steps_here, tile_rows * tile_cols, GROUPS, channels // GROUPS)
    grouped_d = d_norm.reshape(group_shape)
    grouped_n = normal_field.reshape(group_shape)
    cell_count = group_count(tile_rows, tile_cols, channels)
    plain_sum, cross_sum = lax.psum(
        (jnp.sum(grouped_d, axis=(1, 3)), jnp.sum(grouped_d * grouped_n, axis=(1, 3))), ("sy", "sx")
    )
    plain_mean = plain_sum / cell_count
    cross_mean = cross_sum / cell_count
    d_group = (
        grouped_d - plain_mean[:, None, :, None] - grouped_n * cross_mean[:, None, :, None]
    ) * inv_std[:, None, :, None]
    return (upstream + d_group.reshape(upstream.shape), grad_piece)


def shards(
    latent_init,
    step_noise,
    coef_state,
    coef_drift,
    coef_noise,
    step_index,
    time_table,
    norm_gain,
    conv_weight,
    reward_grad,
):
    tile_rows, tile_cols = (step_noise.shape[1], step_noise.shape[2])
    table_ids = jnp.arange(time_table.shape[0], dtype=jnp.int32)
    one_hot = (step_index[:, None] == table_ids[None, :]).astype(jnp.float32)
    embedded = jnp.dot(one_hot, time_table, precision=lax.Precision.HIGHEST)
    modulate = norm_gain[None, :] * (1.0 + embedded)
    state_c = coef_state[:, None, None, None]
    drift_c = coef_drift[:, None, None, None]
    noise_c = coef_noise[:, None, None, None]
    states = jnp.broadcast_to(latent_init[None], step_noise.shape)
    saved_states = []
    caches = []
    trajectory = states
    for sweep_index in range(ITERS):
        saved_states.append(states)
        act_cache = prepare(states, modulate)
        caches.append(act_cache)
        drift_term = states + convolve(act_cache[3], conv_weight, tile_rows, tile_cols)
        increment = (
            state_c * states + drift_c * drift_term + noise_c * step_noise.astype(jnp.float32)
        )
        running = jnp.cumsum(increment, axis=0)
        offset = lower_total(running[-1], False)
        trajectory = latent_init[None] + (offset[None] + running)
        if sweep_index + 1 < ITERS:
            before = jnp.concatenate([jnp.zeros_like(running[:1]), running[:-1]], axis=0)
            states = latent_init[None] + (offset[None] + before)
    adjoint = jnp.broadcast_to(reward_grad[None], step_noise.shape)
    grad_total = jnp.zeros(conv_weight.shape, jnp.float32)
    for sweep_index in range(ITERS - 1, -1, -1):
        act_cache = prepare(saved_states[sweep_index], modulate)
        upstream = drift_c * adjoint
        d_state, grad_piece = backprop(upstream, act_cache, modulate, conv_weight, sweep_index > 0)
        grad_total = grad_total + grad_piece
        if sweep_index > 0:
            through = state_c * adjoint + d_state
            suffix = jnp.cumsum(through[::-1], axis=0)[::-1]
            higher = lower_total(suffix[0], True)
            after = jnp.concatenate([suffix[1:], jnp.zeros_like(suffix[:1])], axis=0)
            adjoint = higher[None] + after
    share = lax.psum_scatter(grad_total, "tm", scatter_dimension=3, tiled=True)
    grad_weight = lax.psum(share, ("sy", "sx"))
    return (trajectory, grad_weight)


def solution(mesh):
    placed = (
        P("sy", "sx", None),
        P("tm", "sy", "sx", None),
        P("tm"),
        P("tm"),
        P("tm"),
        P("tm"),
        P(),
        P(),
        P(),
        P("sy", "sx", None),
    )
    return jax.shard_map(
        shards,
        mesh=mesh,
        in_specs=placed,
        out_specs=(P("tm", "sy", "sx", None), P(None, None, None, "tm")),
        check_vma=False,
    )
```

profile of v0, /device:TPU:0, one launch (start us, length us, event | category | flops | bytes accessed | tf_op | source)
XLA Modules:
  0.0 634.3 jit_solution(18137577999258617183)
XLA Ops:
  8.7 42.0 %psum.46 = f32[4,32]{1,0:T(4,128)S(1)} all-reduce(f32[4,32]{1,0:T(4,128)S(1)} %reduce_sum.117), channel_id=1, replica_groups=mesh['tm'=8,'sy'=4,'sx'=4] {'sy','sx'}, use_global_device_ids=true, to_apply=%region_2.0 | all-reduce | flops 128 | bytes 1024 | tf_op jit(solution)/shard_map/psum | solution.py:52
  52.5 35.5 %psum.49 = f32[4,32]{1,0:T(4,128)S(1)} all-reduce(f32[4,32]{1,0:T(4,128)S(1)} %reduce_sum.120), channel_id=1, replica_groups=mesh['tm'=8,'sy'=4,'sx'=4] {'sy','sx'}, use_global_device_ids=true, to_apply=%region_5.6 | all-reduce | flops 128 | bytes 1024 | tf_op jit(solution)/shard_map/psum | solution.py:55
  93.1 2.6 fusion.164
  95.8 2.3 collective-permute-done.1
  98.3 3.9 collective-permute-start.2
  102.2 1.8 collective-permute-start.3
  106.1 2.8 collective-permute-done.3
  111.1 2.5 fusion.134
  113.6 2.4 fusion.131
  116.0 2.4 fusion.137
  118.4 2.4 fusion.140
  120.8 2.4 fusion.143
  123.3 6.3 fusion.33
  132.3 2.3 collective-permute-start.8
  135.9 3.3 fusion
  139.2 1.6 collective-permute-done.9
  142.3 4.7 collective-permute-start.11
  147.1 3.3 fusion.48
  150.3 2.3 fusion.52
  155.1 2.3 fusion.69
  157.4 2.3 fusion.73
  159.7 2.3 fusion.71
  162.0 2.3 fusion.75
  164.3 2.3 fusion.77
  166.6 8.7 %while.42 = (s32[]{:T(128)}, f32[16,24,320]{2,1,0:T(8,128)S(1)}, s32[]{:T(128)}, f32[8,16,24,320]{3,2,1,0:T(8,128)}, s32[]{:T(128)}, /*index=5*/s32[]{:T(128)}) while((s32[]{:T(128)}, f32[16,24,320]{2,1,0:T(8,128)S(1)}, s32[]{:T(128)}, f32[8,16,24,320]{3,2,1,0:T(8,128)}, s32[]{:T(128)}, /*index=5*/s32[]{:T(128)}) %tuple.106), condition=%wide.region_8.9_spmd.clone, body=%wide.region_7.8_spmd.clone.sunk | while | flops 368644 | bytes 1474653 | solution.py:23
  177.3 39.5 %psum.50 = f32[4,32]{1,0:T(4,128)S(1)} all-reduce(f32[4,32]{1,0:T(4,128)S(1)} %reduce_sum.123), channel_id=1, replica_groups=mesh['tm'=8,'sy'=4,'sx'=4] {'sy','sx'}, use_global_device_ids=true, to_apply=%region_11.12 | all-reduce | flops 128 | bytes 1024 | tf_op jit(solution)/shard_map/psum | solution.py:52
  222.4 36.1 %psum.51 = f32[4,32]{1,0:T(4,128)} all-reduce(f32[4,32]{1,0:T(4,128)} %reduce_sum.126), channel_id=1, replica_groups=mesh['tm'=8,'sy'=4,'sx'=4] {'sy','sx'}, use_global_device_ids=true, to_apply=%region_14.15 | all-reduce | flops 128 | bytes 1024 | tf_op jit(solution)/shard_map/psum | solution.py:55
  261.5 11.5 %fusion.219 = (f32[4,320]{1,0:T(4,128)}, f32[4,320]{1,0:T(4,128)}, f32[4,16,24,320]{3,2,1,0:T(8,128)}) fusion(f32[4,320]{1,0:T(4,128)} %mul.201, f32[4,320]{1,0:T(4,128)S(1)} %sub.66, f32[3,16,24,320]{3,2,1,0:T(8,128)S(1)} %slice.280, f32[16,24,320]{2,1,0:T(8,128)S(1)} %get-tuple-element.239, f32[16,24,320]{2,1,0:T(8,128)S(1)} %copy-done.2, ...), kind=kOutput, calls=%fused_computation.276 | convolution fusion | flops 326858240 | bytes 24750080 | tf_op jit(solution)/shard_map/bhwd,cd->bhwc/dot_general | solution.py:110
  278.9 38.4 %all-reduce.3 = (f32[4,32]{1,0:T(4,128)}, f32[4,32]{1,0:T(4,128)}) all-reduce(f32[4,32]{1,0:T(4,128)} %reduce_sum.132, f32[4,32]{1,0:T(4,128)} %reduce_sum.129), channel_id=1, replica_groups=mesh['tm'=8,'sy'=4,'sx'=4] {'sy','sx'}, use_global_device_ids=true, to_apply=%region_23.24 | all-reduce | flops 256 | bytes 2048 | tf_op jit(solution)/shard_map/psum | solution.py:122
  319.2 1.5 mul.215
  322.1 1.5 sub.72
  323.7 5.2 fusion.18
  328.9 3.3 rev.7
  332.1 1.8 fusion.223
  336.3 1.6 fusion.221
  337.9 1.9 collective-permute-start.4
  341.3 3.2 fusion.60
  344.5 3.5 fusion.162
  349.3 2.8 slice.270
  353.7 1.8 collective-permute-start.6
  356.8 3.8 fusion.146
  360.6 1.6 fusion.57
  362.3 1.6 fusion.63
  363.9 3.3 fusion.145
  367.2 2.2 maximum_maximum_fusion.1
  378.1 3.4 fusion.110
  381.5 4.9 rev.8
  386.4 8.7 %while.44 = (s32[]{:T(128)}, f32[16,24,320]{2,1,0:T(8,128)S(1)}, s32[]{:T(128)}, f32[8,16,24,320]{3,2,1,0:T(8,128)}, s32[]{:T(128)}, /*index=5*/s32[]{:T(128)}) while((s32[]{:T(128)}, f32[16,24,320]{2,1,0:T(8,128)S(1)}, s32[]{:T(128)}, f32[8,16,24,320]{3,2,1,0:T(8,128)}, s32[]{:T(128)}, /*index=5*/s32[]{:T(128)}) %tuple.112), condition=%wide.region_26.27_spmd.clone, body=%wide.region_25.26_spmd.clone.sunk | while | flops 368644 | bytes 1474653 | solution.py:23
  395.1 2.1 multiply_convert_fusion.11
  407.7 2.4 maximum_add_fusion
  410.1 8.4 %copy.14 = f32[3,3,320,320]{2,1,0,3:T(4,128)} copy(f32[3,3,320,320]{3,2,1,0:T(8,128)} %maximum_add_fusion) | data formatting | bytes 7372800 | tf_op jit(solution)/shard_map/add | solution.py:177
  419.1 3.9 fusion.113
  423.0 3.6 fusion.116
  426.6 3.4 fusion.119
  430.0 3.5 fusion.122
  433.5 3.4 fusion.125
  436.9 8.6 %fusion.19 = f32[4,16,24,320]{3,2,1,0:T(8,128)S(1)} fusion(f32[4,16,24,320]{3,2,1,0:T(8,128)} %fusion.110, f32[4,16,24,320]{3,2,1,0:T(8,128)} %fusion.145, f32[4,16,24,320]{3,2,1,0:T(8,128)} %fusion.113, f32[4,16,24,320]{3,2,1,0:T(8,128)} %fusion.116, f32[4,16,24,320]{3,2,1,0:T(8,128)} %fusion.162, f32[4,16,24,320]{3,2,1,0:T(8,128)} %fusion.119, ...), kind=kOutput, calls=%fused_computation.31 | output fusion | flops 9830400 | bytes 23101488 | tf_op jit(solution)/shard_map/jit(cumsum)/reduce_window_sum | solution.py:165
  449.1 50.9 %all-reduce.9.cloned.1.call-done = f32[3,3,320,320]{2,1,0,3:T(4,128)} async-done(((f32[3,3,320,320]{2,1,0,3:T(4,128)}), f32[3,3,320,320]{2,1,0,3:T(4,128)}) %all-reduce.9.cloned.1.call-update) | async-done | bytes 3686416
  500.1 2.1 constant_dynamic-slice_fusion
  502.2 33.7 %all-gather.6.cloned.1.call-done = f32[8,16,24,320]{3,2,1,0:T(8,128)} async-done(((f32[1,16,24,320]{3,2,1,0:T(8,128)}), f32[8,16,24,320]{3,2,1,0:T(8,128)}) %all-gather.6.cloned.1.call-update) | async-done | bytes 3932176 | tf_op jit(solution)/shard_map/all_gather | solution.py:13
  535.9 8.7 %while.43 = (s32[]{:T(128)}, f32[16,24,320]{2,1,0:T(8,128)S(1)}, s32[]{:T(128)}, f32[8,16,24,320]{3,2,1,0:T(8,128)}, s32[]{:T(128)}, /*index=5*/s32[]{:T(128)}) while((s32[]{:T(128)}, f32[16,24,320]{2,1,0:T(8,128)S(1)}, s32[]{:T(128)}, f32[8,16,24,320]{3,2,1,0:T(8,128)}, s32[]{:T(128)}, /*index=5*/s32[]{:T(128)}) %tuple.109), condition=%wide.region_17.18_spmd.clone, body=%wide.region_16.17_spmd.clone.sunk | while | flops 368644 | bytes 1474653 | solution.py:23
  544.6 3.4 add_add_fusion
  548.0 77.7 %all-reduce.7.cloned.1.call-done = f32[3,3,320,40]{2,1,0,3:T(4,128)} async-done(((f32[3,3,320,40]{2,1,0,3:T(4,128)}), f32[3,3,320,40]{2,1,0,3:T(4,128)}) %all-reduce.7.cloned.1.call-update) | async-done | bytes 460816 | tf_op jit(solution)/shard_map/psum | solution.py:185
  625.7 2.0 copy.15
  (223 shorter events, 96.3 us)
Async XLA Ops:
  7.2 81.0 %copy-start = (f32[1000,320]{0,1:T(8,128)S(1)}, f32[1000,320]{0,1:T(8,128)}, u32[]{:S(2)}) copy-start(f32[1000,320]{0,1:T(8,128)} %param.22) | copy-start | bytes 3840004
  7.2 82.6 %copy-start.2 = (f32[16,24,320]{2,1,0:T(8,128)S(1)}, f32[16,24,320]{2,1,0:T(8,128)}, u32[]{:S(2)}) copy-start(f32[16,24,320]{2,1,0:T(8,128)} %param.16) | copy-start | bytes 1474564
  7.2 159.4 %all-gather.4.cloned.1.call-start = ((), (), s32[]{:S(2)}) async-start(), calls=%async_computation | async-start | bytes 5308416 | tf_op jit(solution)/shard_map/all_gather | solution.py:13
  51.0 44.8 %copy-start.39 = (f32[4,320]{1,0:T(4,128)}, f32[4,320]{1,0:T(4,128)S(1)}, u32[]{:S(2)}) copy-start(f32[4,320]{1,0:T(4,128)S(1)} %sub.62) | copy-start | bytes 15364
  88.2 7.5 %copy-start.41 = (f32[4,320]{1,0:T(4,128)}, f32[4,320]{1,0:T(4,128)S(1)}, u32[]{:S(2)}) copy-start(f32[4,320]{1,0:T(4,128)S(1)} %mul.187) | copy-start | bytes 15364
  88.2 4.9 copy-start.9
  90.5 18.4 %copy-start.5 = (bf16[4,16,24,320]{3,2,1,0:T(8,128)(2,1)}, bf16[4,16,24,320]{3,2,1,0:T(8,128)(2,1)S(1)}, u32[]{:S(2)}) copy-start(bf16[4,16,24,320]{3,2,1,0:T(8,128)(2,1)S(1)} %fusion.17) | copy-start | bytes 2949124
  90.5 5.2 collective-permute-start
  91.8 6.2 collective-permute-start.1
  95.8 13.1 %copy-start.32 = (bf16[4,1,24,320]{3,2,1,0:T(8,128)(2,1)}, bf16[4,1,24,320]{3,2,1,0:T(8,128)(2,1)S(1)}, u32[]{:S(2)}) copy-start(bf16[4,1,24,320]{3,2,1,0:T(8,128)(2,1)S(1)} %collective-permute-done) | copy-start | bytes 184324
  98.1 10.8 %copy-start.30 = (bf16[4,1,24,320]{3,2,1,0:T(8,128)(2,1)}, bf16[4,1,24,320]{3,2,1,0:T(8,128)(2,1)S(1)}, u32[]{:S(2)}) copy-start(bf16[4,1,24,320]{3,2,1,0:T(8,128)(2,1)S(1)} %collective-permute-done.1) | copy-start | bytes 184324
  98.3 7.8 %collective-permute-start.2 = (bf16[4,18,1,320]{3,2,1,0:T(2,128)(2,1)S(1)}, bf16[4,18,1,320]{3,2,1,0:T(2,128)(2,1)S(1)}, u32[]{:S(2)}, u32[]{:S(2)}) collective-permute-start(bf16[4,18,1,320]{3,2,1,0:T(2,128)(2,1)S(1)} %get-tuple-element.333), channel_id=1, source_target_pairs={{0,1},{1,2},{2,3},{4,5},{5,6},{6,7},{8,9},{9,10},{10,11},{12,13},{... | collective-permute-start | bytes 138248 | tf_op jit(solution)/shard_map/ppermute | solution.py:31
  102.2 6.6 %collective-permute-start.3 = (bf16[4,18,1,320]{3,2,1,0:T(2,128)(2,1)S(1)}, bf16[4,18,1,320]{3,2,1,0:T(2,128)(2,1)S(1)}, u32[]{:S(2)}, u32[]{:S(2)}) collective-permute-start(bf16[4,18,1,320]{3,2,1,0:T(2,128)(2,1)S(1)} %get-tuple-element.334), channel_id=1, source_target_pairs={{1,0},{2,1},{3,2},{5,4},{6,5},{7,6},{9,8},{10,9},{11,10},{13,12},{... | collective-permute-start | bytes 138248 | tf_op jit(solution)/shard_map/ppermute | solution.py:34
  110.0 8.3 %copy-start.11 = (bf16[4,18,25,320]{3,2,1,0:T(8,128)(2,1)}, bf16[4,18,25,320]{3,2,1,0:T(8,128)(2,1)S(1)}, u32[]{:S(2)}) copy-start(bf16[4,18,25,320]{3,2,1,0:T(8,128)(2,1)S(1)} %get-tuple-element.332) | copy-start | bytes 3456004
  110.0 10.8 %copy-start.13 = (bf16[4,18,25,320]{3,2,1,0:T(8,128)(2,1)}, bf16[4,18,25,320]{3,2,1,0:T(8,128)(2,1)S(1)}, u32[]{:S(2)}) copy-start(bf16[4,18,25,320]{3,2,1,0:T(8,128)(2,1)S(1)} %get-tuple-element.331) | copy-start | bytes 3456004
  120.8 2.4 copy-start.43
  120.8 2.4 copy-start.45
  120.8 2.4 copy-start.47
  123.3 8.7 %copy-start.28 = (f32[16,24,320]{2,1,0:T(8,128)S(1)}, f32[16,24,320]{2,1,0:T(8,128)}, u32[]{:S(2)}) copy-start(f32[16,24,320]{2,1,0:T(8,128)} %param.25) | copy-start | bytes 1474564
  129.6 1.4 copy-start.23
  131.9 249.6 %all-gather.8.cloned.1.call-start = ((), (), s32[]{:S(2)}) async-start(), calls=%async_computation.2 | async-start | bytes 5308416 | tf_op jit(solution)/shard_map/all_gather | solution.py:13
  132.3 18.0 %copy-start.7 = (bf16[4,16,24,320]{3,2,1,0:T(8,128)(2,1)}, bf16[4,16,24,320]{3,2,1,0:T(8,128)(2,1)S(1)}, u32[]{:S(2)}) copy-start(bf16[4,16,24,320]{3,2,1,0:T(8,128)(2,1)S(1)} %multiply_convert_fusion) | copy-start | bytes 2949124
  132.3 6.9 %collective-permute-start.8 = (bf16[4,1,24,320]{3,2,1,0:T(8,128)(2,1)S(1)}, bf16[4,1,24,320]{3,2,1,0:T(8,128)(2,1)S(1)}, u32[]{:S(2)}, u32[]{:S(2)}) collective-permute-start(bf16[4,1,24,320]{3,2,1,0:T(8,128)(2,1)S(1)} %get-tuple-element.336), channel_id=1, source_target_pairs={{0,4},{4,8},{8,12},{1,5},{5,9},{9,13},{2,6},{6,10},{10,14},{3,7},{... | collective-permute-start | bytes 184328 | tf_op jit(solution)/shard_map/ppermute | solution.py:31
  134.6 6.2 collective-permute-start.9
  139.2 11.1 %copy-start.10 = (bf16[3,3,320,320]{3,2,1,0:T(8,128)(2,1)S(1)}, bf16[3,3,320,320]{3,2,1,0:T(8,128)(2,1)}, u32[]{:S(2)}) copy-start(bf16[3,3,320,320]{3,2,1,0:T(8,128)(2,1)} %param.24) | copy-start | bytes 5529604
  139.2 11.1 %copy-start.34 = (bf16[4,1,24,320]{3,2,1,0:T(8,128)(2,1)}, bf16[4,1,24,320]{3,2,1,0:T(8,128)(2,1)S(1)}, u32[]{:S(2)}) copy-start(bf16[4,1,24,320]{3,2,1,0:T(8,128)(2,1)S(1)} %collective-permute-done.8) | copy-start | bytes 184324
  140.8 9.5 %copy-start.36 = (bf16[4,1,24,320]{3,2,1,0:T(8,128)(2,1)}, bf16[4,1,24,320]{3,2,1,0:T(8,128)(2,1)S(1)}, u32[]{:S(2)}) copy-start(bf16[4,1,24,320]{3,2,1,0:T(8,128)(2,1)S(1)} %collective-permute-done.9) | copy-start | bytes 184324
  141.0 11.8 %collective-permute-start.10 = (bf16[4,18,1,320]{3,2,1,0:T(2,128)(2,1)S(1)}, bf16[4,18,1,320]{3,2,1,0:T(2,128)(2,1)S(1)}, u32[]{:S(2)}, u32[]{:S(2)}) collective-permute-start(bf16[4,18,1,320]{3,2,1,0:T(2,128)(2,1)S(1)} %get-tuple-element.326), channel_id=1, source_target_pairs={{1,0},{2,1},{3,2},{5,4},{6,5},{7,6},{9,8},{10,9},{11,10},{13,12},{... | collective-permute-start | bytes 138248 | tf_op jit(solution)/shard_map/ppermute | solution.py:34
  142.3 10.5 %collective-permute-start.11 = (bf16[4,18,1,320]{3,2,1,0:T(2,128)(2,1)S(1)}, bf16[4,18,1,320]{3,2,1,0:T(2,128)(2,1)S(1)}, u32[]{:S(2)}, u32[]{:S(2)}) collective-permute-start(bf16[4,18,1,320]{3,2,1,0:T(2,128)(2,1)S(1)} %get-tuple-element.325), channel_id=1, source_target_pairs={{0,1},{1,2},{2,3},{4,5},{5,6},{6,7},{8,9},{9,10},{10,11},{12,13},{... | collective-permute-start | bytes 138248 | tf_op jit(solution)/shard_map/ppermute | solution.py:31
  150.3 2.4 copy-start.24
  152.7 1.3 copy-start.8
  152.7 1.3 copy-start.35
  152.7 1.3 copy-start.37
  155.1 6.9 %copy-start.19 = (bf16[4,18,25,320]{3,2,1,0:T(8,128)(2,1)}, bf16[4,18,25,320]{3,2,1,0:T(8,128)(2,1)S(1)}, u32[]{:S(2)}) copy-start(bf16[4,18,25,320]{3,2,1,0:T(8,128)(2,1)S(1)} %get-tuple-element.323) | copy-start | bytes 3456004
  332.1 9.1 %copy-start.44 = (f32[4]{0:T(128)S(1)}, f32[4]{0:T(128)}, u32[]{:S(2)}) copy-start(f32[4]{0:T(128)} %param.19) | copy-start | bytes 52
  334.0 1.4 copy-start.21
  336.3 163.8 %all-reduce.9.cloned.1.call-start = ((), (), s32[]{:S(2)}) async-start(), calls=%async_computation.4 | async-start | bytes 11796480
  337.9 14.2 %collective-permute-start.4 = (bf16[4,1,24,320]{3,2,1,0:T(8,128)(2,1)}, bf16[4,1,24,320]{3,2,1,0:T(8,128)(2,1)}, u32[]{:S(2)}, u32[]{:S(2)}) collective-permute-start(bf16[4,1,24,320]{3,2,1,0:T(8,128)(2,1)} %get-tuple-element.337), channel_id=1, source_target_pairs={{0,4},{4,8},{8,12},{1,5},{5,9},{9,13},{2,6},{6,10},{10,14},{3,7},{... | collective-permute-start | bytes 184328 | tf_op jit(solution)/shard_map/ppermute | solution.py:31
  339.8 4.7 copy-start.3
  339.8 12.3 %collective-permute-start.5 = (bf16[4,1,24,320]{3,2,1,0:T(8,128)(2,1)}, bf16[4,1,24,320]{3,2,1,0:T(8,128)(2,1)}, u32[]{:S(2)}, u32[]{:S(2)}) collective-permute-start(bf16[4,1,24,320]{3,2,1,0:T(8,128)(2,1)} %get-tuple-element.338), channel_id=1, source_target_pairs={{4,0},{8,4},{12,8},{5,1},{9,5},{13,9},{6,2},{10,6},{14,10},{7,3},{... | collective-permute-start | bytes 184328 | tf_op jit(solution)/shard_map/ppermute | solution.py:34
  344.5 3.5 copy-start.22
  352.2 8.4 %copy-start.4 = (bf16[4,16,24,320]{3,2,1,0:T(8,128)(2,1)S(1)}, bf16[4,16,24,320]{3,2,1,0:T(8,128)(2,1)}, u32[]{:S(2)}) copy-start(bf16[4,16,24,320]{3,2,1,0:T(8,128)(2,1)} %get-tuple-element.322) | copy-start | bytes 2949124
  352.2 8.4 %copy-start.29 = (f32[16,24,320]{2,1,0:T(8,128)S(1)}, f32[16,24,320]{2,1,0:T(8,128)}, u32[]{:S(2)}) copy-start(f32[16,24,320]{2,1,0:T(8,128)} %param.25) | copy-start | bytes 1474564
  353.7 13.6 %collective-permute-start.6 = (bf16[4,18,1,320]{3,2,1,0:T(2,128)(2,1)S(1)}, bf16[4,18,1,320]{3,2,1,0:T(2,128)(2,1)S(1)}, u32[]{:S(2)}, u32[]{:S(2)}) collective-permute-start(bf16[4,18,1,320]{3,2,1,0:T(2,128)(2,1)S(1)} %get-tuple-element.329), channel_id=1, source_target_pairs={{0,1},{1,2},{2,3},{4,5},{5,6},{6,7},{8,9},{9,10},{10,11},{12,13},{... | collective-permute-start | bytes 138248 | tf_op jit(solution)/shard_map/ppermute | solution.py:31
  355.5 11.8 %collective-permute-start.7 = (bf16[4,18,1,320]{3,2,1,0:T(2,128)(2,1)S(1)}, bf16[4,18,1,320]{3,2,1,0:T(2,128)(2,1)S(1)}, u32[]{:S(2)}, u32[]{:S(2)}) collective-permute-start(bf16[4,18,1,320]{3,2,1,0:T(2,128)(2,1)S(1)} %get-tuple-element.330), channel_id=1, source_target_pairs={{1,0},{2,1},{3,2},{5,4},{6,5},{7,6},{9,8},{10,9},{11,10},{13,12},{... | collective-permute-start | bytes 138248 | tf_op jit(solution)/shard_map/ppermute | solution.py:34
  369.5 5.8 copy-start.15
  369.5 8.6 %copy-start.17 = (bf16[4,18,25,320]{3,2,1,0:T(8,128)(2,1)}, bf16[4,18,25,320]{3,2,1,0:T(8,128)(2,1)S(1)}, u32[]{:S(2)}) copy-start(bf16[4,18,25,320]{3,2,1,0:T(8,128)(2,1)S(1)} %get-tuple-element.328) | copy-start | bytes 3456004
  373.0 1.0 copy-start.38
  395.0 2.1 copy-start.12
  397.1 1.5 copy-start.14
  402.6 1.3 copy-start.6
  402.6 1.3 copy-start.33
  405.4 1.4 copy-start.25
  405.4 1.8 copy-start.26
  405.4 2.3 copy-start.27
  418.5 117.4 %all-gather.6.cloned.1.call-start = ((), (), s32[]{:S(2)}) async-start(), calls=%async_computation.1 | async-start | bytes 5308416 | tf_op jit(solution)/shard_map/all_gather | solution.py:13
  419.1 3.9 copy-start.18
  423.0 3.6 copy-start.16
  433.5 3.4 copy-start.46
  433.5 3.4 copy-start.48
  436.9 11.0 %copy-start.49 = (u32[128]{0:T(128)S(1)}, u32[128]{0:T(128)}, u32[]{:S(2)}) copy-start(u32[128]{0:T(128)} %constant.115) | copy-start | bytes 1540
  445.5 1.4 copy-start.20
  447.8 177.9 %all-reduce.7.cloned.1.call-start = ((), (), s32[]{:S(2)}) async-start(), calls=%async_computation.3 | async-start | bytes 1474560 | tf_op jit(solution)/shard_map/psum | solution.py:185
  544.6 83.0 %copy-start.1 = (f32[1000,320]{0,1:T(8,128)S(1)}, f32[1000,320]{0,1:T(8,128)}, u32[]{:S(2)}) copy-start(f32[1000,320]{0,1:T(8,128)} %param.22) | copy-start | bytes 3840004
  (3 other events, 2.4 us)
Sparse Core Ops, SparseCore 0:
  132.0 33.4 all-gather.3
  336.4 29.2 all-gather.7
  418.7 81.3 all-reduce.8
  501.7 34.1 all-gather.5
  539.4 86.2 all-reduce.6
where the time goes:
time: 641 us; the launch traced here: 634 us
  blocking collectives  191 us (30%)
  waiting for transfers between devices  169 us (26%)
  matrix products  101 us (16%)
  other arithmetic  78.4 us (12%)
  local copies, waits for them, and re-layouts  53.7 us (8%)
  starting transfers between devices  24.9 us (4%)
  between operations  15.4 us (2%)
    psum x2, blocking collectives, group_stats(): totals = lax.psum(jnp.sum(grouped, axis=(1, 3)), ('sy', 'sx'))  81.5 us
    psum x1, waiting for transfers between devices, shards(): grad_weight = lax.psum(share, ('sy', 'sx'))  77.7 us
    psum x2, blocking collectives, group_stats(): lax.psum(jnp.sum(shifted * shifted, axis=(1, 3)), ('sy', 'sx')) / cell_count  71.6 us
    unnamed x6, waiting for transfers between devices  51 us
    dot_general x18, matrix products, convolve(): jnp.einsum('bhwc,cd->bhwd', window, conv_weight[row_off, col_off], prefer...  49.6 us
    psum x1, blocking collectives, backprop(): lax.psum((jnp.sum(grouped_d, axis=(1, 3)), jnp.sum(grouped_d * grouped_n,...  38.4 us
    all_gather x3, waiting for transfers between devices, prefix(): pieces = lax.all_gather(value, axis)  33.7 us
    dot_general x9, matrix products, backprop(): jnp.einsum('bhwd,cd->bhwc', window, conv_weight[row_off, col_off], prefer...  31.9 us
  transfers between devices with their start and end apart: 17, of which 6 were waited for; matrix products, arithmetic and copies ran while one was open for 17% of the time, Pallas kernels for 0%

commit v1 on v0

--- a/solution.py
+++ b/solution.py
@@ -52,7 +52,7 @@
     totals = lax.psum(jnp.sum(grouped, axis=(1, 3)), ("sy", "sx"))
     center = totals / cell_count
     shifted = grouped - center[:, None, :, None]
-    spread = lax.psum(jnp.sum(shifted * shifted, axis=(1, 3)), ("sy", "sx")) / cell_count
+    spread = lax.psum(lax.psum(jnp.sum(shifted * shifted, axis=(1, 3)), "sy"), "sx") / cell_count
     return (shifted, spread)
 
 

time: 641 us -> 605 us (0.944)
  blocking collectives: 191 us -> 153 us
    psum x2 -> x4, blocking collectives: 71.6 us -> 32.9 us  [the longest x2 16.7 us: group_stats(): lax.psum(lax.psum(jnp.sum(shifted * shifted, axis=(1, 3)), 'sy'), 'sx')]
  transfers between devices with their start and end apart: 17 -> 17, of which waited for: 6 -> 6; matrix products, arithmetic and copies ran while one was open for 17% -> 18% of each run, Pallas kernels for 0% -> 0%
where the time goes in v1:
time: 605 us; the launch traced here: 598 us
  waiting for transfers between devices  170 us (28%)
  blocking collectives  153 us (25%)
  matrix products  101 us (17%)
  other arithmetic  78.5 us (13%)
  local copies, waits for them, and re-layouts  53.6 us (9%)
  starting transfers between devices  26.5 us (4%)
  between operations  15.5 us (3%)
    psum x2, blocking collectives, group_stats(): totals = lax.psum(jnp.sum(grouped, axis=(1, 3)), ('sy', 'sx'))  80.4 us
    psum x1, waiting for transfers between devices, shards(): grad_weight = lax.psum(share, ('sy', 'sx'))  77.7 us
    unnamed x6, waiting for transfers between devices  51.7 us
    dot_general x18, matrix products, convolve(): jnp.einsum('bhwc,cd->bhwd', window, conv_weight[row_off, col_off], prefer...  49.5 us
    psum x1, blocking collectives, backprop(): lax.psum((jnp.sum(grouped_d, axis=(1, 3)), jnp.sum(grouped_d * grouped_n,...  39.5 us
    all_gather x3, waiting for transfers between devices, prefix(): pieces = lax.all_gather(value, axis)  33.7 us
    dot_general x9, matrix products, backprop(): jnp.einsum('bhwd,cd->bhwc', window, conv_weight[row_off, col_off], prefer...  31.9 us
    select_n x21, other arithmetic, step(): return jnp.where(position < mine, longer, subtotal)  25.6 us
  transfers between devices with their start and end apart: 17, of which 6 were waited for; matrix products, arithmetic and copies ran while one was open for 18% of the time, Pallas kernels for 0%

profile of v1, /device:TPU:0, one launch (start us, length us, event | category | flops | bytes accessed | tf_op | source)
XLA Modules:
  0.0 597.8 jit_solution(12280209810786141959)
XLA Ops:
  8.7 42.0 %psum.60 = f32[4,32]{1,0:T(4,128)S(1)} all-reduce(f32[4,32]{1,0:T(4,128)S(1)} %reduce_sum.117), channel_id=1, replica_groups=mesh['tm'=8,'sy'=4,'sx'=4] {'sy','sx'}, use_global_device_ids=true, to_apply=%region_2.0 | all-reduce | flops 128 | bytes 1024 | tf_op jit(solution)/shard_map/psum | solution.py:52
  52.5 7.7 %psum.61 = f32[4,32]{1,0:T(4,128)S(1)} all-reduce(f32[4,32]{1,0:T(4,128)S(1)} %reduce_sum.120), channel_id=1, replica_groups=mesh['tm'=8,'sy'=4,'sx'=4] {'sy'}, use_global_device_ids=true, to_apply=%region_5.6 | all-reduce | flops 128 | bytes 1024 | tf_op jit(solution)/shard_map/psum | solution.py:55
  60.3 8.0 %psum.64 = f32[4,32]{1,0:T(4,128)S(1)} all-reduce(f32[4,32]{1,0:T(4,128)S(1)} %psum.61), channel_id=1, replica_groups=mesh['tm'=8,'sy'=4,'sx'=4] {'sx'}, use_global_device_ids=true, to_apply=%region_6.7 | all-reduce | flops 128 | bytes 1024 | tf_op jit(solution)/shard_map/psum | solution.py:55
  70.8 3.6 collective-permute-start
  75.8 2.6 fusion.164
  78.4 2.3 collective-permute-done.1
  80.9 3.9 collective-permute-start.2
  84.8 1.8 collective-permute-start.3
  88.7 2.8 collective-permute-done.3
  93.7 2.5 fusion.134
  96.2 2.4 fusion.131
  98.6 2.4 fusion.137
  101.0 2.5 fusion.140
  103.5 2.4 fusion.143
  105.9 6.3 %fusion.33 = f32[4,16,24,320]{3,2,1,0:T(8,128)S(1)} fusion(bf16[4,16,24,320]{3,2,1,0:T(8,128)(2,1)} %param.17, f32[4,16,24,320]{3,2,1,0:T(8,128)S(1)} %fusion.128, f32[4,16,24,320]{3,2,1,0:T(8,128)S(1)} %fusion.147, f32[4,16,24,320]{3,2,1,0:T(8,128)} %fusion.131, f32[4,16,24,320]{3,2,1,0:T(8,128)} %fusion.134, f32[4,16,24,320]{3,2,1,0:T(8,128)} %fusion.164, ...), kind=kOutput, calls=%fused_computation.49 | output fusion | flops 8847360 | bytes 21135408 | tf_op jit(solution)/shard_map/jit(cumsum)/reduce_window_sum | solution.py:165
  114.9 2.3 collective-permute-start.8
  118.5 3.3 fusion
  121.9 1.6 collective-permute-done.9
  125.0 4.7 collective-permute-start.11
  129.7 3.2 fusion.48
  132.9 2.4 fusion.52
  137.7 2.3 fusion.69
  140.0 2.3 fusion.73
  142.3 2.3 fusion.71
  144.6 2.3 fusion.75
  146.9 2.3 fusion.77
  149.2 8.7 %while.42 = (s32[]{:T(128)}, f32[16,24,320]{2,1,0:T(8,128)S(1)}, s32[]{:T(128)}, f32[8,16,24,320]{3,2,1,0:T(8,128)}, s32[]{:T(128)}, /*index=5*/s32[]{:T(128)}) while((s32[]{:T(128)}, f32[16,24,320]{2,1,0:T(8,128)S(1)}, s32[]{:T(128)}, f32[8,16,24,320]{3,2,1,0:T(8,128)}, s32[]{:T(128)}, /*index=5*/s32[]{:T(128)}) %tuple.106), condition=%wide.region_9.10_spmd.clone, body=%wide.region_8.9_spmd.clone.sunk | while | flops 368644 | bytes 1474653 | solution.py:23
  159.8 38.4 %psum.65 = f32[4,32]{1,0:T(4,128)S(1)} all-reduce(f32[4,32]{1,0:T(4,128)S(1)} %reduce_sum.123), channel_id=1, replica_groups=mesh['tm'=8,'sy'=4,'sx'=4] {'sy','sx'}, use_global_device_ids=true, to_apply=%region_12.13 | all-reduce | flops 128 | bytes 1024 | tf_op jit(solution)/shard_map/psum | solution.py:52
  203.9 8.4 %psum.66 = f32[4,32]{1,0:T(4,128)} all-reduce(f32[4,32]{1,0:T(4,128)} %reduce_sum.126), channel_id=1, replica_groups=mesh['tm'=8,'sy'=4,'sx'=4] {'sy'}, use_global_device_ids=true, to_apply=%region_15.16 | all-reduce | flops 128 | bytes 1024 | tf_op jit(solution)/shard_map/psum | solution.py:55
  212.3 8.7 %psum.69 = f32[4,32]{1,0:T(4,128)} all-reduce(f32[4,32]{1,0:T(4,128)} %psum.66), channel_id=1, replica_groups=mesh['tm'=8,'sy'=4,'sx'=4] {'sx'}, use_global_device_ids=true, to_apply=%region_16.17 | all-reduce | flops 128 | bytes 1024 | tf_op jit(solution)/shard_map/psum | solution.py:55
  224.0 11.5 %fusion.219 = (f32[4,320]{1,0:T(4,128)}, f32[4,320]{1,0:T(4,128)}, f32[4,16,24,320]{3,2,1,0:T(8,128)}) fusion(f32[4,320]{1,0:T(4,128)} %mul.201, f32[4,320]{1,0:T(4,128)S(1)} %sub.66, f32[3,16,24,320]{3,2,1,0:T(8,128)S(1)} %slice.280, f32[16,24,320]{2,1,0:T(8,128)S(1)} %get-tuple-element.239, f32[16,24,320]{2,1,0:T(8,128)S(1)} %copy-done.2, ...), kind=kOutput, calls=%fused_computation.276 | convolution fusion | flops 326858240 | bytes 24750080 | tf_op jit(solution)/shard_map/bhwd,cd->bhwc/dot_general | solution.py:110
  241.3 39.5 %all-reduce.3 = (f32[4,32]{1,0:T(4,128)}, f32[4,32]{1,0:T(4,128)}) all-reduce(f32[4,32]{1,0:T(4,128)} %reduce_sum.132, f32[4,32]{1,0:T(4,128)} %reduce_sum.129), channel_id=1, replica_groups=mesh['tm'=8,'sy'=4,'sx'=4] {'sy','sx'}, use_global_device_ids=true, to_apply=%region_25.26 | all-reduce | flops 256 | bytes 2048 | tf_op jit(solution)/shard_map/psum | solution.py:122
  287.3 5.2 fusion.18
  292.5 3.3 rev.7
  295.8 1.8 fusion.223
  299.9 1.6 fusion.221
  301.5 1.9 collective-permute-start.4
  304.9 3.3 fusion.60
  308.2 3.5 fusion.162
  313.0 2.8 slice.270
  319.9 3.8 fusion.146
  323.8 1.6 fusion.57
  325.4 1.6 fusion.63
  327.0 3.4 fusion.145
  330.4 2.4 maximum_maximum_fusion.1
  341.4 3.4 fusion.110
  344.8 4.9 rev.8
  349.7 8.7 %while.44 = (s32[]{:T(128)}, f32[16,24,320]{2,1,0:T(8,128)S(1)}, s32[]{:T(128)}, f32[8,16,24,320]{3,2,1,0:T(8,128)}, s32[]{:T(128)}, /*index=5*/s32[]{:T(128)}) while((s32[]{:T(128)}, f32[16,24,320]{2,1,0:T(8,128)S(1)}, s32[]{:T(128)}, f32[8,16,24,320]{3,2,1,0:T(8,128)}, s32[]{:T(128)}, /*index=5*/s32[]{:T(128)}) %tuple.112), condition=%wide.region_28.29_spmd.clone, body=%wide.region_27.28_spmd.clone.sunk | while | flops 368644 | bytes 1474653 | solution.py:23
  358.4 2.1 multiply_convert_fusion.11
  371.0 2.3 maximum_add_fusion
  373.3 8.4 %copy.14 = f32[3,3,320,320]{2,1,0,3:T(4,128)} copy(f32[3,3,320,320]{3,2,1,0:T(8,128)} %maximum_add_fusion) | data formatting | bytes 7372800 | tf_op jit(solution)/shard_map/add | solution.py:177
  382.0 3.9 fusion.113
  385.9 3.5 fusion.116
  389.4 3.4 fusion.119
  392.8 3.5 fusion.122
  396.3 3.4 fusion.125
  399.7 8.6 %fusion.19 = f32[4,16,24,320]{3,2,1,0:T(8,128)S(1)} fusion(f32[4,16,24,320]{3,2,1,0:T(8,128)} %fusion.110, f32[4,16,24,320]{3,2,1,0:T(8,128)} %fusion.145, f32[4,16,24,320]{3,2,1,0:T(8,128)} %fusion.113, f32[4,16,24,320]{3,2,1,0:T(8,128)} %fusion.116, f32[4,16,24,320]{3,2,1,0:T(8,128)} %fusion.162, f32[4,16,24,320]{3,2,1,0:T(8,128)} %fusion.119, ...), kind=kOutput, calls=%fused_computation.31 | output fusion | flops 9830400 | bytes 23101488 | tf_op jit(solution)/shard_map/jit(cumsum)/reduce_window_sum | solution.py:165
  411.9 51.7 %all-reduce.9.cloned.1.call-done = f32[3,3,320,320]{2,1,0,3:T(4,128)} async-done(((f32[3,3,320,320]{2,1,0,3:T(4,128)}), f32[3,3,320,320]{2,1,0,3:T(4,128)}) %all-reduce.9.cloned.1.call-update) | async-done | bytes 3686416
  463.6 2.1 constant_dynamic-slice_fusion
  465.7 33.7 %all-gather.6.cloned.1.call-done = f32[8,16,24,320]{3,2,1,0:T(8,128)} async-done(((f32[1,16,24,320]{3,2,1,0:T(8,128)}), f32[8,16,24,320]{3,2,1,0:T(8,128)}) %all-gather.6.cloned.1.call-update) | async-done | bytes 3932176 | tf_op jit(solution)/shard_map/all_gather | solution.py:13
  499.4 8.7 %while.43 = (s32[]{:T(128)}, f32[16,24,320]{2,1,0:T(8,128)S(1)}, s32[]{:T(128)}, f32[8,16,24,320]{3,2,1,0:T(8,128)}, s32[]{:T(128)}, /*index=5*/s32[]{:T(128)}) while((s32[]{:T(128)}, f32[16,24,320]{2,1,0:T(8,128)S(1)}, s32[]{:T(128)}, f32[8,16,24,320]{3,2,1,0:T(8,128)}, s32[]{:T(128)}, /*index=5*/s32[]{:T(128)}) %tuple.109), condition=%wide.region_19.20_spmd.clone, body=%wide.region_18.19_spmd.clone.sunk | while | flops 368644 | bytes 1474653 | solution.py:23
  508.1 3.4 add_add_fusion
  511.4 77.7 %all-reduce.7.cloned.1.call-done = f32[3,3,320,40]{2,1,0,3:T(4,128)} async-done(((f32[3,3,320,40]{2,1,0,3:T(4,128)}), f32[3,3,320,40]{2,1,0,3:T(4,128)}) %all-reduce.7.cloned.1.call-update) | async-done | bytes 460816 | tf_op jit(solution)/shard_map/psum | solution.py:185
  589.1 2.0 copy.15
  (225 shorter events, 99.0 us)
Async XLA Ops:
  7.2 61.3 %copy-start = (f32[1000,320]{0,1:T(8,128)S(1)}, f32[1000,320]{0,1:T(8,128)}, u32[]{:S(2)}) copy-start(f32[1000,320]{0,1:T(8,128)} %param.22) | copy-start | bytes 3840004
  7.2 62.9 %copy-start.2 = (f32[16,24,320]{2,1,0:T(8,128)S(1)}, f32[16,24,320]{2,1,0:T(8,128)}, u32[]{:S(2)}) copy-start(f32[16,24,320]{2,1,0:T(8,128)} %param.16) | copy-start | bytes 1474564
  7.2 142.0 %all-gather.4.cloned.1.call-start = ((), (), s32[]{:S(2)}) async-start(), calls=%async_computation | async-start | bytes 5308416 | tf_op jit(solution)/shard_map/all_gather | solution.py:13
  51.0 27.4 %copy-start.39 = (f32[4,320]{1,0:T(4,128)}, f32[4,320]{1,0:T(4,128)S(1)}, u32[]{:S(2)}) copy-start(f32[4,320]{1,0:T(4,128)S(1)} %sub.62) | copy-start | bytes 15364
  68.5 9.9 %copy-start.41 = (f32[4,320]{1,0:T(4,128)}, f32[4,320]{1,0:T(4,128)S(1)}, u32[]{:S(2)}) copy-start(f32[4,320]{1,0:T(4,128)S(1)} %mul.187) | copy-start | bytes 15364
  68.5 7.2 %copy-start.9 = (bf16[3,3,320,320]{3,2,1,0:T(8,128)(2,1)S(1)}, bf16[3,3,320,320]{3,2,1,0:T(8,128)(2,1)}, u32[]{:S(2)}) copy-start(bf16[3,3,320,320]{3,2,1,0:T(8,128)(2,1)} %param.24) | copy-start | bytes 5529604
  70.8 20.7 %copy-start.5 = (bf16[4,16,24,320]{3,2,1,0:T(8,128)(2,1)}, bf16[4,16,24,320]{3,2,1,0:T(8,128)(2,1)S(1)}, u32[]{:S(2)}) copy-start(bf16[4,16,24,320]{3,2,1,0:T(8,128)(2,1)S(1)} %fusion.17) | copy-start | bytes 2949124
  70.8 7.6 %collective-permute-start = (bf16[4,1,24,320]{3,2,1,0:T(8,128)(2,1)S(1)}, bf16[4,1,24,320]{3,2,1,0:T(8,128)(2,1)S(1)}, u32[]{:S(2)}, u32[]{:S(2)}) collective-permute-start(bf16[4,1,24,320]{3,2,1,0:T(8,128)(2,1)S(1)} %get-tuple-element.339), channel_id=1, source_target_pairs={{0,4},{4,8},{8,12},{1,5},{5,9},{9,13},{2,6},{6,10},{10,14},{3,7},{... | collective-permute-start | bytes 184328 | tf_op jit(solution)/shard_map/ppermute | solution.py:31
  74.5 6.2 %collective-permute-start.1 = (bf16[4,1,24,320]{3,2,1,0:T(8,128)(2,1)S(1)}, bf16[4,1,24,320]{3,2,1,0:T(8,128)(2,1)S(1)}, u32[]{:S(2)}, u32[]{:S(2)}) collective-permute-start(bf16[4,1,24,320]{3,2,1,0:T(8,128)(2,1)S(1)} %get-tuple-element.340), channel_id=1, source_target_pairs={{4,0},{8,4},{12,8},{5,1},{9,5},{13,9},{6,2},{10,6},{14,10},{7,3},{... | collective-permute-start | bytes 184328 | tf_op jit(solution)/shard_map/ppermute | solution.py:34
  78.4 13.1 %copy-start.32 = (bf16[4,1,24,320]{3,2,1,0:T(8,128)(2,1)}, bf16[4,1,24,320]{3,2,1,0:T(8,128)(2,1)S(1)}, u32[]{:S(2)}) copy-start(bf16[4,1,24,320]{3,2,1,0:T(8,128)(2,1)S(1)} %collective-permute-done) | copy-start | bytes 184324
  80.7 10.8 %copy-start.30 = (bf16[4,1,24,320]{3,2,1,0:T(8,128)(2,1)}, bf16[4,1,24,320]{3,2,1,0:T(8,128)(2,1)S(1)}, u32[]{:S(2)}) copy-start(bf16[4,1,24,320]{3,2,1,0:T(8,128)(2,1)S(1)} %collective-permute-done.1) | copy-start | bytes 184324
  80.9 7.7 %collective-permute-start.2 = (bf16[4,18,1,320]{3,2,1,0:T(2,128)(2,1)S(1)}, bf16[4,18,1,320]{3,2,1,0:T(2,128)(2,1)S(1)}, u32[]{:S(2)}, u32[]{:S(2)}) collective-permute-start(bf16[4,18,1,320]{3,2,1,0:T(2,128)(2,1)S(1)} %get-tuple-element.333), channel_id=1, source_target_pairs={{0,1},{1,2},{2,3},{4,5},{5,6},{6,7},{8,9},{9,10},{10,11},{12,13},{... | collective-permute-start | bytes 138248 | tf_op jit(solution)/shard_map/ppermute | solution.py:31
  84.8 6.6 %collective-permute-start.3 = (bf16[4,18,1,320]{3,2,1,0:T(2,128)(2,1)S(1)}, bf16[4,18,1,320]{3,2,1,0:T(2,128)(2,1)S(1)}, u32[]{:S(2)}, u32[]{:S(2)}) collective-permute-start(bf16[4,18,1,320]{3,2,1,0:T(2,128)(2,1)S(1)} %get-tuple-element.334), channel_id=1, source_target_pairs={{1,0},{2,1},{3,2},{5,4},{6,5},{7,6},{9,8},{10,9},{11,10},{13,12},{... | collective-permute-start | bytes 138248 | tf_op jit(solution)/shard_map/ppermute | solution.py:34
  92.6 8.4 %copy-start.11 = (bf16[4,18,25,320]{3,2,1,0:T(8,128)(2,1)}, bf16[4,18,25,320]{3,2,1,0:T(8,128)(2,1)S(1)}, u32[]{:S(2)}) copy-start(bf16[4,18,25,320]{3,2,1,0:T(8,128)(2,1)S(1)} %get-tuple-element.332) | copy-start | bytes 3456004
  92.6 10.8 %copy-start.13 = (bf16[4,18,25,320]{3,2,1,0:T(8,128)(2,1)}, bf16[4,18,25,320]{3,2,1,0:T(8,128)(2,1)S(1)}, u32[]{:S(2)}) copy-start(bf16[4,18,25,320]{3,2,1,0:T(8,128)(2,1)S(1)} %get-tuple-element.331) | copy-start | bytes 3456004
  103.5 2.4 copy-start.43
  103.5 2.4 copy-start.45
  103.5 2.4 copy-start.47
  105.9 8.7 %copy-start.28 = (f32[16,24,320]{2,1,0:T(8,128)S(1)}, f32[16,24,320]{2,1,0:T(8,128)}, u32[]{:S(2)}) copy-start(f32[16,24,320]{2,1,0:T(8,128)} %param.25) | copy-start | bytes 1474564
  112.2 1.4 copy-start.23
  114.5 230.3 %all-gather.8.cloned.1.call-start = ((), (), s32[]{:S(2)}) async-start(), calls=%async_computation.2 | async-start | bytes 5308416 | tf_op jit(solution)/shard_map/all_gather | solution.py:13
  114.9 18.0 %copy-start.7 = (bf16[4,16,24,320]{3,2,1,0:T(8,128)(2,1)}, bf16[4,16,24,320]{3,2,1,0:T(8,128)(2,1)S(1)}, u32[]{:S(2)}) copy-start(bf16[4,16,24,320]{3,2,1,0:T(8,128)(2,1)S(1)} %multiply_convert_fusion) | copy-start | bytes 2949124
  114.9 6.9 %collective-permute-start.8 = (bf16[4,1,24,320]{3,2,1,0:T(8,128)(2,1)S(1)}, bf16[4,1,24,320]{3,2,1,0:T(8,128)(2,1)S(1)}, u32[]{:S(2)}, u32[]{:S(2)}) collective-permute-start(bf16[4,1,24,320]{3,2,1,0:T(8,128)(2,1)S(1)} %get-tuple-element.336), channel_id=1, source_target_pairs={{0,4},{4,8},{8,12},{1,5},{5,9},{9,13},{2,6},{6,10},{10,14},{3,7},{... | collective-permute-start | bytes 184328 | tf_op jit(solution)/shard_map/ppermute | solution.py:31
  117.2 6.2 %collective-permute-start.9 = (bf16[4,1,24,320]{3,2,1,0:T(8,128)(2,1)S(1)}, bf16[4,1,24,320]{3,2,1,0:T(8,128)(2,1)S(1)}, u32[]{:S(2)}, u32[]{:S(2)}) collective-permute-start(bf16[4,1,24,320]{3,2,1,0:T(8,128)(2,1)S(1)} %get-tuple-element.335), channel_id=1, source_target_pairs={{4,0},{8,4},{12,8},{5,1},{9,5},{13,9},{6,2},{10,6},{14,10},{7,3},{... | collective-permute-start | bytes 184328 | tf_op jit(solution)/shard_map/ppermute | solution.py:34
  121.8 11.1 %copy-start.10 = (bf16[3,3,320,320]{3,2,1,0:T(8,128)(2,1)S(1)}, bf16[3,3,320,320]{3,2,1,0:T(8,128)(2,1)}, u32[]{:S(2)}) copy-start(bf16[3,3,320,320]{3,2,1,0:T(8,128)(2,1)} %param.24) | copy-start | bytes 5529604
  121.9 11.0 %copy-start.34 = (bf16[4,1,24,320]{3,2,1,0:T(8,128)(2,1)}, bf16[4,1,24,320]{3,2,1,0:T(8,128)(2,1)S(1)}, u32[]{:S(2)}) copy-start(bf16[4,1,24,320]{3,2,1,0:T(8,128)(2,1)S(1)} %collective-permute-done.8) | copy-start | bytes 184324
  123.5 9.4 %copy-start.36 = (bf16[4,1,24,320]{3,2,1,0:T(8,128)(2,1)}, bf16[4,1,24,320]{3,2,1,0:T(8,128)(2,1)S(1)}, u32[]{:S(2)}) copy-start(bf16[4,1,24,320]{3,2,1,0:T(8,128)(2,1)S(1)} %collective-permute-done.9) | copy-start | bytes 184324
  123.7 11.8 %collective-permute-start.10 = (bf16[4,18,1,320]{3,2,1,0:T(2,128)(2,1)S(1)}, bf16[4,18,1,320]{3,2,1,0:T(2,128)(2,1)S(1)}, u32[]{:S(2)}, u32[]{:S(2)}) collective-permute-start(bf16[4,18,1,320]{3,2,1,0:T(2,128)(2,1)S(1)} %get-tuple-element.326), channel_id=1, source_target_pairs={{1,0},{2,1},{3,2},{5,4},{6,5},{7,6},{9,8},{10,9},{11,10},{13,12},{... | collective-permute-start | bytes 138248 | tf_op jit(solution)/shard_map/ppermute | solution.py:34
  125.0 10.5 %collective-permute-start.11 = (bf16[4,18,1,320]{3,2,1,0:T(2,128)(2,1)S(1)}, bf16[4,18,1,320]{3,2,1,0:T(2,128)(2,1)S(1)}, u32[]{:S(2)}, u32[]{:S(2)}) collective-permute-start(bf16[4,18,1,320]{3,2,1,0:T(2,128)(2,1)S(1)} %get-tuple-element.325), channel_id=1, source_target_pairs={{0,1},{1,2},{2,3},{4,5},{5,6},{6,7},{8,9},{9,10},{10,11},{12,13},{... | collective-permute-start | bytes 138248 | tf_op jit(solution)/shard_map/ppermute | solution.py:31
  132.9 2.4 copy-start.24
  135.3 1.3 copy-start.8
  135.3 1.3 copy-start.35
  135.3 1.3 copy-start.37
  137.7 6.9 %copy-start.19 = (bf16[4,18,25,320]{3,2,1,0:T(8,128)(2,1)}, bf16[4,18,25,320]{3,2,1,0:T(8,128)(2,1)S(1)}, u32[]{:S(2)}) copy-start(bf16[4,18,25,320]{3,2,1,0:T(8,128)(2,1)S(1)} %get-tuple-element.323) | copy-start | bytes 3456004
  295.8 9.1 %copy-start.44 = (f32[4]{0:T(128)S(1)}, f32[4]{0:T(128)}, u32[]{:S(2)}) copy-start(f32[4]{0:T(128)} %param.19) | copy-start | bytes 52
  297.6 1.4 copy-start.21
  299.9 163.7 %all-reduce.9.cloned.1.call-start = ((), (), s32[]{:S(2)}) async-start(), calls=%async_computation.4 | async-start | bytes 11796480
  301.5 14.3 %collective-permute-start.4 = (bf16[4,1,24,320]{3,2,1,0:T(8,128)(2,1)}, bf16[4,1,24,320]{3,2,1,0:T(8,128)(2,1)}, u32[]{:S(2)}, u32[]{:S(2)}) collective-permute-start(bf16[4,1,24,320]{3,2,1,0:T(8,128)(2,1)} %get-tuple-element.337), channel_id=1, source_target_pairs={{0,4},{4,8},{8,12},{1,5},{5,9},{9,13},{2,6},{6,10},{10,14},{3,7},{... | collective-permute-start | bytes 184328 | tf_op jit(solution)/shard_map/ppermute | solution.py:31
  303.5 4.7 copy-start.3
  303.5 12.4 %collective-permute-start.5 = (bf16[4,1,24,320]{3,2,1,0:T(8,128)(2,1)}, bf16[4,1,24,320]{3,2,1,0:T(8,128)(2,1)}, u32[]{:S(2)}, u32[]{:S(2)}) collective-permute-start(bf16[4,1,24,320]{3,2,1,0:T(8,128)(2,1)} %get-tuple-element.338), channel_id=1, source_target_pairs={{4,0},{8,4},{12,8},{5,1},{9,5},{13,9},{6,2},{10,6},{14,10},{7,3},{... | collective-permute-start | bytes 184328 | tf_op jit(solution)/shard_map/ppermute | solution.py:34
  308.2 3.5 copy-start.22
  315.8 7.9 %copy-start.4 = (bf16[4,16,24,320]{3,2,1,0:T(8,128)(2,1)S(1)}, bf16[4,16,24,320]{3,2,1,0:T(8,128)(2,1)}, u32[]{:S(2)}) copy-start(bf16[4,16,24,320]{3,2,1,0:T(8,128)(2,1)} %get-tuple-element.322) | copy-start | bytes 2949124
  315.8 7.9 %copy-start.29 = (f32[16,24,320]{2,1,0:T(8,128)S(1)}, f32[16,24,320]{2,1,0:T(8,128)}, u32[]{:S(2)}) copy-start(f32[16,24,320]{2,1,0:T(8,128)} %param.25) | copy-start | bytes 1474564
  317.3 13.1 %collective-permute-start.6 = (bf16[4,18,1,320]{3,2,1,0:T(2,128)(2,1)S(1)}, bf16[4,18,1,320]{3,2,1,0:T(2,128)(2,1)S(1)}, u32[]{:S(2)}, u32[]{:S(2)}) collective-permute-start(bf16[4,18,1,320]{3,2,1,0:T(2,128)(2,1)S(1)} %get-tuple-element.329), channel_id=1, source_target_pairs={{0,1},{1,2},{2,3},{4,5},{5,6},{6,7},{8,9},{9,10},{10,11},{12,13},{... | collective-permute-start | bytes 138248 | tf_op jit(solution)/shard_map/ppermute | solution.py:31
  318.6 11.8 %collective-permute-start.7 = (bf16[4,18,1,320]{3,2,1,0:T(2,128)(2,1)S(1)}, bf16[4,18,1,320]{3,2,1,0:T(2,128)(2,1)S(1)}, u32[]{:S(2)}, u32[]{:S(2)}) collective-permute-start(bf16[4,18,1,320]{3,2,1,0:T(2,128)(2,1)S(1)} %get-tuple-element.330), channel_id=1, source_target_pairs={{1,0},{2,1},{3,2},{5,4},{6,5},{7,6},{9,8},{10,9},{11,10},{13,12},{... | collective-permute-start | bytes 138248 | tf_op jit(solution)/shard_map/ppermute | solution.py:34
  332.8 5.8 copy-start.15
  332.8 8.6 %copy-start.17 = (bf16[4,18,25,320]{3,2,1,0:T(8,128)(2,1)}, bf16[4,18,25,320]{3,2,1,0:T(8,128)(2,1)S(1)}, u32[]{:S(2)}) copy-start(bf16[4,18,25,320]{3,2,1,0:T(8,128)(2,1)S(1)} %get-tuple-element.328) | copy-start | bytes 3456004
  336.4 1.0 copy-start.38
  358.4 2.1 copy-start.12
  360.5 1.5 copy-start.14
  365.9 1.3 copy-start.6
  365.9 1.3 copy-start.33
  368.8 1.4 copy-start.25
  368.8 1.8 copy-start.26
  368.8 2.3 copy-start.27
  381.7 117.7 %all-gather.6.cloned.1.call-start = ((), (), s32[]{:S(2)}) async-start(), calls=%async_computation.1 | async-start | bytes 5308416 | tf_op jit(solution)/shard_map/all_gather | solution.py:13
  381.9 3.9 copy-start.18
  385.9 3.5 copy-start.16
  396.3 3.4 copy-start.46
  396.3 3.4 copy-start.48
  399.7 11.0 %copy-start.49 = (u32[128]{0:T(128)S(1)}, u32[128]{0:T(128)}, u32[]{:S(2)}) copy-start(u32[128]{0:T(128)} %constant.115) | copy-start | bytes 1540
  408.3 1.4 copy-start.20
  410.6 178.6 %all-reduce.7.cloned.1.call-start = ((), (), s32[]{:S(2)}) async-start(), calls=%async_computation.3 | async-start | bytes 1474560 | tf_op jit(solution)/shard_map/psum | solution.py:185
  508.1 83.0 %copy-start.1 = (f32[1000,320]{0,1:T(8,128)S(1)}, f32[1000,320]{0,1:T(8,128)}, u32[]{:S(2)}) copy-start(f32[1000,320]{0,1:T(8,128)} %param.22) | copy-start | bytes 3840004
  (3 other events, 2.3 us)
Sparse Core Ops, SparseCore 0:
  114.6 32.3 all-gather.3
  300.0 29.2 all-gather.7
  381.8 81.6 all-reduce.8
  465.2 34.1 all-gather.5
  502.9 86.2 all-reduce.6
